TPU v7x, 32 devices: a whole 2x2x4 slice. The times are simulated.
32 devices in a mesh: gx: 8 (over y, x, core), gy: 4 (over z).
Axes of the slice: x: 2, y: 2, z: 4, core: 2. Of those that a mesh axis runs over, the one named last changes fastest.
Arguments:
- provisional: bfloat16 [4, 8, 1024, 1024], P(None, 'gx', 'gy'), may hold values from -6 to 6
- implicit_terms: bfloat16 [4, 8, 1024, 1024], P(None, 'gx', 'gy'), may hold values from -6 to 6
- adv_speed: float32 [8, 1024], P('gx'), may hold values from 0.2 to 1.2
- reaction: float32 [8, 1024], P('gx'), may hold values from 0.1 to 2
- wall_rate: float32 [1024], replicated, may hold values from 0.05 to 20
- span_rate: float32 [1024], replicated, may hold values from 0.01 to 4
- analysis: bfloat16 [1024, 1024], replicated, may hold values from -1 to 2
- synthesis: bfloat16 [1024, 1024], replicated, may hold values from -1 to 2
Outputs:
- end_value: float32 [8, 1024, 1024], P('gx', 'gy')
All inputs are finite; a program needn't handle non-finite values.
Results may differ from a plain program's by a relative error of at most 0.0063.
Values may be sent and summed in bfloat16 or wider, within the bound.
A program may use at most 64 MiB of HBM per device.

v0:
```python
import math
import jax
import jax.numpy as jnp
from jax import lax
from jax.sharding import PartitionSpec as P


def spectral_weights():
    root_five = math.sqrt(5.0)
    points = [0.0, 0.5 - 0.5 / root_five, 0.5 + 0.5 / root_five, 1.0]
    gauss_offset = 1.0 / math.sqrt(3.0)
    weights = [[0.0, 0.0, 0.0, 0.0] for m in range(3)]
    for m in range(3):
        half_width = 0.5 * (points[m + 1] - points[m])
        centre = 0.5 * (points[m + 1] + points[m])
        for sign_factor in (-1.0, 1.0):
            sample = centre + half_width * sign_factor * gauss_offset
            for j in range(4):
                basis_value = 1.0
                for i in range(4):
                    if i != j:
                        basis_value = basis_value * (sample - points[i]) / (points[j] - points[i])
                weights[m][j] = weights[m][j] + half_width * basis_value
    return (points, weights)


def shifted(cells, axis):
    count = lax.axis_size(axis)
    behind = lax.ppermute(cells, axis, [(i, (i + 1) % count) for i in range(count)])
    forward = lax.ppermute(cells, axis, [((i + 1) % count, i) for i in range(count)])
    return forward.astype(jnp.float32) - behind.astype(jnp.float32)


def per_device(
    provisional, implicit_terms, adv_speed, reaction, wall_rate, span_rate, analysis, synthesis
):
    points, weights = spectral_weights()
    steps = [float(points[m + 1] - points[m]) for m in range(3)]
    modes_dev = span_rate.shape[0] // lax.axis_size("gy")
    span_part = lax.dynamic_slice_in_dim(span_rate, lax.axis_index("gy") * modes_dev, modes_dev, 0)
    rows_dev = provisional.shape[2]
    row_start = lax.axis_index("gy") * rows_dev
    half_speed = 0.5 * adv_speed[0][:, None]
    decay = reaction[0][:, None]
    half_speed_part = lax.dynamic_slice_in_dim(half_speed, row_start, rows_dev, 0)
    decay_part = lax.dynamic_slice_in_dim(decay, row_start, rows_dev, 0)
    prov = [provisional[j, 0].astype(jnp.float32) for j in range(4)]
    impl = [implicit_terms[j, 0].astype(jnp.float32) for j in range(4)]
    known = []
    for m in range(3):
        field_weights = [weights[m][j] - (steps[m] if m == j and m > 0 else 0.0) for j in range(4)]
        impl_weights = [weights[m][j] - (steps[m] if j == m + 1 else 0.0) for j in range(4)]
        mixed = sum((float(field_weights[j]) * prov[j] for j in range(4)))
        local = sum((float(impl_weights[j]) * impl[j] for j in range(4))) - decay_part * mixed
        if m == 0:
            local = local + prov[0]
        local = local - half_speed_part * shifted(mixed.astype(jnp.bfloat16), "gx")
        known.append(local.astype(jnp.bfloat16))
    known = [
        lax.all_to_all(field, "gy", split_axis=1, concat_axis=0, tiled=True) for field in known
    ]
    for m in range(3):
        rhs = known[m].astype(jnp.float32)
        if m:
            sent = current.astype(jnp.bfloat16)
            rhs = (
                rhs
                + current
                - steps[m] * (decay * sent.astype(jnp.float32) + half_speed * shifted(sent, "gx"))
            )
        factors = 1.0 / (1.0 + steps[m] * (wall_rate[:, None] + span_part[None, :]))
        coefficients = jnp.dot(
            analysis, rhs.astype(jnp.bfloat16), preferred_element_type=jnp.float32
        )
        scaled = (coefficients * factors).astype(jnp.bfloat16)
        current = jnp.dot(synthesis, scaled, preferred_element_type=jnp.float32)
    result = lax.all_to_all(
        current.astype(jnp.bfloat16), "gy", split_axis=0, concat_axis=1, tiled=True
    )
    return result.astype(jnp.float32)[None]


def solution(mesh):
    placed = (
        P(None, "gx", "gy", None),
        P(None, "gx", "gy", None),
        P("gx", None),
        P("gx", None),
        P(),
        P(),
        P(),
        P(),
    )
    return jax.shard_map(
        per_device, mesh=mesh, in_specs=placed, out_specs=P("gx", "gy", None), check_vma=False
    )
```

profile of v0, /device:TPU:3, one launch (start us, length us, event | category | flops | bytes accessed | tf_op | source)
XLA Modules:
  0.0 144.3 jit_solution(17562041078309248272)
XLA Ops:
  0.0 2.8 %fusion.85 = (bf16[1,1,256,1024]{3,2,1,0:T(8,128)(2,1)S(1)}, bf16[1,1,256,1024]{3,2,1,0:T(8,128)(2,1)}, bf16[1,1,256,1024]{3,2,1,0:T(8,128)(2,1)}, bf16[1,1,256,1024]{3,2,1,0:T(8,128)(2,1)}) fusion(bf16[4,1,256,1024]{3,2,1,0:T(8,128)(2,1)} %param.8), kind=kLoop, calls=%fused_computation.115 | loop fusion | bytes 4194304 | tf_op jit(solution)/shard_map/slice | solution.py:47
  2.8 0.2 copy.44
  3.0 1.2 copy.45
  4.3 2.1 %copy.46 = bf16[1,1,256,1024]{2,3,1,0:T(8,128)(2,1)} copy(bf16[1,1,256,1024]{3,2,1,0:T(8,128)(2,1)} %get-tuple-element.12) | data formatting | bytes 1048576
  6.4 2.1 %copy.47 = bf16[1,1,256,1024]{2,3,1,0:T(8,128)(2,1)} copy(bf16[1,1,256,1024]{3,2,1,0:T(8,128)(2,1)} %get-tuple-element.14) | data formatting | bytes 1048576
  8.4 3.1 %fusion.76 = (bf16[256,1024]{0,1:T(8,128)(2,1)}, bf16[256,1024]{0,1:T(8,128)(2,1)}, bf16[256,1024]{0,1:T(8,128)(2,1)}) fusion(bf16[1,1,256,1024]{2,3,1,0:T(8,128)(2,1)} %copy.47, bf16[1,1,256,1024]{2,3,1,0:T(8,128)(2,1)} %copy.46, bf16[1,1,256,1024]{2,3,1,0:T(8,128)(2,1)S(1)} %copy.45, bf16[1,1,256,1024]{2,3,1,0:T(8,128)(2,1)S(1)} %copy.44), kind=kLoop, calls=%fused_computation.105 | loop fusion | flops 7340032 | bytes 3670016 | tf_op jit(solution)/shard_map/convert_element_type | solution.py:57
  11.6 0.7 collective-permute-start
  12.2 2.0 %collective-permute-start.1 = (bf16[256,1024]{0,1:T(8,128)(2,1)}, bf16[256,1024]{0,1:T(8,128)(2,1)}, u32[]{:S(2)}, u32[]{:S(2)}) collective-permute-start(bf16[256,1024]{0,1:T(8,128)(2,1)} %get-tuple-element.8), channel_id=1, source_target_pairs={{0,4},{4,8},{8,12},{12,16},{16,20},{20,24},{24,28},{28,0},{1,5},{5... | collective-permute-start | bytes 1572872 | tf_op jit(solution)/shard_map/ppermute | solution.py:29
  14.2 2.6 %collective-permute-start.3 = (bf16[256,1024]{0,1:T(8,128)(2,1)}, bf16[256,1024]{0,1:T(8,128)(2,1)}, u32[]{:S(2)}, u32[]{:S(2)}) collective-permute-start(bf16[256,1024]{0,1:T(8,128)(2,1)} %get-tuple-element.9), channel_id=1, source_target_pairs={{0,4},{4,8},{8,12},{12,16},{16,20},{20,24},{24,28},{28,0},{1,5},{5... | collective-permute-start | bytes 1572872 | tf_op jit(solution)/shard_map/ppermute | solution.py:29
  16.8 0.0 collective-permute-start.4
  16.9 10.1 %collective-permute-done = bf16[256,1024]{0,1:T(8,128)(2,1)} collective-permute-done((bf16[256,1024]{0,1:T(8,128)(2,1)}, bf16[256,1024]{0,1:T(8,128)(2,1)}, u32[]{:S(2)}, u32[]{:S(2)}) %collective-permute-start) | collective-permute-done | bytes 524320 | tf_op jit(solution)/shard_map/ppermute | solution.py:30
  26.9 0.0 collective-permute-start.5
  26.9 2.9 %fusion.86 = (bf16[1,1,256,1024]{3,2,1,0:T(8,128)(2,1)}, bf16[1,1,256,1024]{3,2,1,0:T(8,128)(2,1)}, bf16[1,1,256,1024]{3,2,1,0:T(8,128)(2,1)}, bf16[1,1,256,1024]{3,2,1,0:T(8,128)(2,1)}) fusion(bf16[4,1,256,1024]{3,2,1,0:T(8,128)(2,1)} %param.9), kind=kLoop, calls=%fused_computation.116 | loop fusion | bytes 4194304 | tf_op jit(solution)/shard_map/slice | solution.py:48
  29.8 2.1 %copy.40 = bf16[1,1,256,1024]{2,3,1,0:T(8,128)(2,1)} copy(bf16[1,1,256,1024]{3,2,1,0:T(8,128)(2,1)} %get-tuple-element.15) | data formatting | bytes 1048576
  31.9 2.0 %copy.41 = bf16[1,1,256,1024]{2,3,1,0:T(8,128)(2,1)} copy(bf16[1,1,256,1024]{3,2,1,0:T(8,128)(2,1)} %get-tuple-element.17) | data formatting | bytes 1048576
  33.9 2.0 %copy.42 = bf16[1,1,256,1024]{2,3,1,0:T(8,128)(2,1)} copy(bf16[1,1,256,1024]{3,2,1,0:T(8,128)(2,1)} %get-tuple-element.16) | data formatting | bytes 1048576
  36.0 2.1 %copy.43 = bf16[1,1,256,1024]{2,3,1,0:T(8,128)(2,1)} copy(bf16[1,1,256,1024]{3,2,1,0:T(8,128)(2,1)} %get-tuple-element.18) | data formatting | bytes 1048576
  38.1 0.0 collective-permute-done.1
  38.1 0.1 collective-permute-done.2
  38.2 0.0 collective-permute-done.3
  38.2 11.2 %collective-permute-done.4 = bf16[256,1024]{0,1:T(8,128)(2,1)} collective-permute-done((bf16[256,1024]{0,1:T(8,128)(2,1)}, bf16[256,1024]{0,1:T(8,128)(2,1)}, u32[]{:S(2)}, u32[]{:S(2)}) %collective-permute-start.4) | collective-permute-done | bytes 524320 | tf_op jit(solution)/shard_map/ppermute | solution.py:30
  49.4 0.0 collective-permute-done.5
  49.4 5.2 %fusion.17 = (bf16[256,1024]{0,1:T(8,128)(2,1)}, bf16[256,1024]{0,1:T(8,128)(2,1)}, bf16[256,1024]{0,1:T(8,128)(2,1)S(1)}) fusion(bf16[1,1,256,1024]{2,3,1,0:T(8,128)(2,1)} %copy.40, bf16[1,1,256,1024]{2,3,1,0:T(8,128)(2,1)} %copy.41, bf16[1,1,256,1024]{2,3,1,0:T(8,128)(2,1)} %copy.42, bf16[1,1,256,1024]{2,3,1,0:T(8,128)(2,1)} %copy.43, ...), kind=kLoop, calls=%fused_computation.49 | loop fusion | flops 19660800 | bytes 8914944 | tf_op jit(solution)/shard_map/convert_element_type | solution.py:58
  54.7 0.0 copy-start.3
  54.7 18.7 %all_to_all.58 = bf16[256,4,256]{0,2,1:T(8,128)(2,1)S(1)} all-to-all(bf16[256,4,256]{0,2,1:T(8,128)(2,1)S(1)} %bitcast.194), channel_id=1, replica_groups=mesh['gx'=8,'gy'=4] {'gy'}, dimensions={1} | all-to-all | bytes 1048576 | tf_op jit(solution)/shard_map/all_to_all | solution.py:60
  73.4 3.5 %all-to-all-start.1 = ((bf16[256,4,256]{0,2,1:T(8,128)(2,1)}), bf16[256,4,256]{0,2,1:T(8,128)(2,1)S(1)}, u32[]{:S(2)}, u32[]{:S(2)}) async-start(bf16[256,4,256]{0,2,1:T(8,128)(2,1)} %bitcast.193), calls=%async_computation.1 | async-start | bytes 1048576 | tf_op jit(solution)/shard_map/all_to_all | solution.py:60
  76.9 0.8 dynamic_slice.11
  77.7 1.0 copy.37
  78.7 4.3 %fusion.87 = (bf16[1024,256]{0,1:T(8,128)(2,1)}, f32[1024,256]{0,1:T(8,128)}) fusion(bf16[1024,1024]{1,0:T(8,128)(2,1)S(1)} %copy-done, bf16[1024,256]{1,0:T(8,128)(2,1)} %bitcast.200, bf16[1024,1024]{1,0:T(8,128)(2,1)} %param.14, f32[256]{0:T(256)S(1)} %dynamic_slice.11, f32[1024]{0:T(1024)S(1)} %copy-done.3), kind=kOutput, calls=%fused_computation.117 | convolution fusion | flops 1075576832 | bytes 6296576 | tf_op jit(solution)/shard_map/dot_general | solution.py:76
  83.0 0.4 collective-permute-start.6
  83.4 2.3 %collective-permute-start.7 = (bf16[1024,256]{0,1:T(8,128)(2,1)}, bf16[1024,256]{0,1:T(8,128)(2,1)}, u32[]{:S(2)}, u32[]{:S(2)}) collective-permute-start(bf16[1024,256]{0,1:T(8,128)(2,1)} %get-tuple-element.19), channel_id=1, source_target_pairs={{0,4},{4,8},{8,12},{12,16},{16,20},{20,24},{24,28},{28,0},{1,5},{5... | collective-permute-start | bytes 1572872 | tf_op jit(solution)/shard_map/ppermute | solution.py:29
  85.7 5.4 %all-to-all-done.1 = bf16[256,4,256]{0,2,1:T(8,128)(2,1)S(1)} async-done(((bf16[256,4,256]{0,2,1:T(8,128)(2,1)}), bf16[256,4,256]{0,2,1:T(8,128)(2,1)S(1)}, u32[]{:S(2)}, u32[]{:S(2)}) %all-to-all-start.1) | async-done | bytes 524320 | tf_op jit(solution)/shard_map/all_to_all | solution.py:60
  91.1 3.5 %all-to-all-start = ((bf16[256,4,256]{0,2,1:T(8,128)(2,1)}), bf16[256,4,256]{0,2,1:T(8,128)(2,1)S(1)}, u32[]{:S(2)}, u32[]{:S(2)}) async-start(bf16[256,4,256]{0,2,1:T(8,128)(2,1)} %bitcast.7), calls=%async_computation | async-start | bytes 1048576 | tf_op jit(solution)/shard_map/all_to_all | solution.py:60
  94.6 0.1 convert_bitcast_fusion
  94.7 1.1 copy.50
  95.8 2.2 %collective-permute-done.6 = bf16[1024,256]{0,1:T(8,128)(2,1)} collective-permute-done((bf16[1024,256]{0,1:T(8,128)(2,1)}, bf16[1024,256]{0,1:T(8,128)(2,1)}, u32[]{:S(2)}, u32[]{:S(2)}) %collective-permute-start.6) | collective-permute-done | bytes 524320 | tf_op jit(solution)/shard_map/ppermute | solution.py:30
  98.0 5.3 %fusion.88 = (bf16[1024,256]{0,1:T(8,128)(2,1)}, f32[1024,256]{0,1:T(8,128)}) fusion(bf16[1024,1024]{1,0:T(8,128)(2,1)S(1)} %copy-done, bf16[1024,1024]{1,0:T(8,128)(2,1)} %param.14, bf16[1024,256]{0,1:T(8,128)(2,1)} %collective-permute-done.7, bf16[1024,256]{0,1:T(8,128)(2,1)} %collective-permute-done.6, bf16[1024,256]{0,1:T(8,128)(2,1)} %get-tuple-element.19, ...), kind=kOutput, calls=%fused_computation.118 | convolution fusion | flops 1078460416 | bytes 9450496 | tf_op jit(solution)/shard_map/dot_general | solution.py:76
  103.3 0.0 collective-permute-start.8
  103.3 2.6 %collective-permute-start.9 = (bf16[1024,256]{0,1:T(8,128)(2,1)}, bf16[1024,256]{0,1:T(8,128)(2,1)}, u32[]{:S(2)}, u32[]{:S(2)}) collective-permute-start(bf16[1024,256]{0,1:T(8,128)(2,1)} %get-tuple-element.21), channel_id=1, source_target_pairs={{0,4},{4,8},{8,12},{12,16},{16,20},{20,24},{24,28},{28,0},{1,5},{5... | collective-permute-start | bytes 1572872 | tf_op jit(solution)/shard_map/ppermute | solution.py:29
  106.0 2.6 %all-to-all-done = bf16[256,4,256]{0,2,1:T(8,128)(2,1)S(1)} async-done(((bf16[256,4,256]{0,2,1:T(8,128)(2,1)}), bf16[256,4,256]{0,2,1:T(8,128)(2,1)S(1)}, u32[]{:S(2)}, u32[]{:S(2)}) %all-to-all-start) | async-done | bytes 524320 | tf_op jit(solution)/shard_map/all_to_all | solution.py:60
  108.5 0.1 convert_bitcast_fusion.1
  108.6 0.1 copy.49
  108.8 8.8 %collective-permute-done.8 = bf16[1024,256]{0,1:T(8,128)(2,1)} collective-permute-done((bf16[1024,256]{0,1:T(8,128)(2,1)}, bf16[1024,256]{0,1:T(8,128)(2,1)}, u32[]{:S(2)}, u32[]{:S(2)}) %collective-permute-start.8) | collective-permute-done | bytes 524320 | tf_op jit(solution)/shard_map/ppermute | solution.py:30
  117.6 4.6 %convolution_convert_fusion = bf16[256,1024]{1,0:T(8,128)(2,1)} fusion(bf16[1024,1024]{1,0:T(8,128)(2,1)S(1)} %copy-done, bf16[1024,1024]{1,0:T(8,128)(2,1)} %param.14, bf16[1024,256]{0,1:T(8,128)(2,1)} %collective-permute-done.9, bf16[1024,256]{0,1:T(8,128)(2,1)} %collective-permute-done.8, bf16[1024,256]{0,1:T(8,128)(2,1)} %get-tuple-element.21, ...), kind=kOutput, calls=%fused_computation.35 | convolution fusion | flops 1078460416 | bytes 8401920 | tf_op jit(solution)/shard_map/dot_general | solution.py:76
  122.2 1.1 copy.52
  123.3 19.6 %all_to_all.59 = bf16[4,256,256]{1,2,0:T(8,128)(2,1)S(1)} all-to-all(bf16[4,256,256]{1,2,0:T(8,128)(2,1)S(1)} %bitcast.196), channel_id=1, replica_groups=mesh['gx'=8,'gy'=4] {'gy'}, dimensions={0} | all-to-all | bytes 1048576 | tf_op jit(solution)/shard_map/all_to_all | solution.py:77
  142.9 0.1 convert_element_type.202
  143.0 1.3 copy.39
  (12 shorter events, 0.0 us)
Async XLA Ops:
  0.0 78.7 %copy-start = (bf16[1024,1024]{1,0:T(8,128)(2,1)S(1)}, bf16[1024,1024]{1,0:T(8,128)(2,1)}, u32[]{:S(2)}) copy-start(bf16[1024,1024]{1,0:T(8,128)(2,1)} %param.15) | copy-start | bytes 6291460
  11.6 15.4 %collective-permute-start = (bf16[256,1024]{0,1:T(8,128)(2,1)}, bf16[256,1024]{0,1:T(8,128)(2,1)}, u32[]{:S(2)}, u32[]{:S(2)}) collective-permute-start(bf16[256,1024]{0,1:T(8,128)(2,1)} %get-tuple-element.8), channel_id=1, source_target_pairs={{4,0},{8,4},{12,8},{16,12},{20,16},{24,20},{28,24},{0,28},{5,1},{9... | collective-permute-start | bytes 1572872 | tf_op jit(solution)/shard_map/ppermute | solution.py:30
  12.2 25.8 %collective-permute-start.1 = (bf16[256,1024]{0,1:T(8,128)(2,1)}, bf16[256,1024]{0,1:T(8,128)(2,1)}, u32[]{:S(2)}, u32[]{:S(2)}) collective-permute-start(bf16[256,1024]{0,1:T(8,128)(2,1)} %get-tuple-element.8), channel_id=1, source_target_pairs={{0,4},{4,8},{8,12},{12,16},{16,20},{20,24},{24,28},{28,0},{1,5},{5... | collective-permute-start | bytes 1572872 | tf_op jit(solution)/shard_map/ppermute | solution.py:29
  14.2 24.0 %collective-permute-start.2 = (bf16[256,1024]{0,1:T(8,128)(2,1)}, bf16[256,1024]{0,1:T(8,128)(2,1)}, u32[]{:S(2)}, u32[]{:S(2)}) collective-permute-start(bf16[256,1024]{0,1:T(8,128)(2,1)} %get-tuple-element.9), channel_id=1, source_target_pairs={{4,0},{8,4},{12,8},{16,12},{20,16},{24,20},{28,24},{0,28},{5,1},{9... | collective-permute-start | bytes 1572872 | tf_op jit(solution)/shard_map/ppermute | solution.py:30
  14.2 24.0 %collective-permute-start.3 = (bf16[256,1024]{0,1:T(8,128)(2,1)}, bf16[256,1024]{0,1:T(8,128)(2,1)}, u32[]{:S(2)}, u32[]{:S(2)}) collective-permute-start(bf16[256,1024]{0,1:T(8,128)(2,1)} %get-tuple-element.9), channel_id=1, source_target_pairs={{0,4},{4,8},{8,12},{12,16},{16,20},{20,24},{24,28},{28,0},{1,5},{5... | collective-permute-start | bytes 1572872 | tf_op jit(solution)/shard_map/ppermute | solution.py:29
  16.8 32.6 %collective-permute-start.4 = (bf16[256,1024]{0,1:T(8,128)(2,1)}, bf16[256,1024]{0,1:T(8,128)(2,1)}, u32[]{:S(2)}, u32[]{:S(2)}) collective-permute-start(bf16[256,1024]{0,1:T(8,128)(2,1)} %get-tuple-element.10), channel_id=1, source_target_pairs={{4,0},{8,4},{12,8},{16,12},{20,16},{24,20},{28,24},{0,28},{5,1},{9... | collective-permute-start | bytes 1572872 | tf_op jit(solution)/shard_map/ppermute | solution.py:30
  26.9 22.5 %collective-permute-start.5 = (bf16[256,1024]{0,1:T(8,128)(2,1)}, bf16[256,1024]{0,1:T(8,128)(2,1)}, u32[]{:S(2)}, u32[]{:S(2)}) collective-permute-start(bf16[256,1024]{0,1:T(8,128)(2,1)} %get-tuple-element.10), channel_id=1, source_target_pairs={{0,4},{4,8},{8,12},{12,16},{16,20},{20,24},{24,28},{28,0},{1,5},{5... | collective-permute-start | bytes 1572872 | tf_op jit(solution)/shard_map/ppermute | solution.py:29
  29.8 8.2 %copy-start.1 = (f32[1,1024]{1,0:T(1,128)S(1)}, f32[1,1024]{1,0:T(1,128)}, u32[]{:S(2)}) copy-start(f32[1,1024]{1,0:T(1,128)} %param.10) | copy-start | bytes 12292
  29.8 8.2 %copy-start.2 = (f32[1,1024]{1,0:T(1,128)S(1)}, f32[1,1024]{1,0:T(1,128)}, u32[]{:S(2)}) copy-start(f32[1,1024]{1,0:T(1,128)} %param.11) | copy-start | bytes 12292
  54.7 24.0 %copy-start.3 = (f32[1024]{0:T(1024)S(1)}, f32[1024]{0:T(1024)}, u32[]{:S(2)}) copy-start(f32[1024]{0:T(1024)} %param.12) | copy-start | bytes 12292
  73.4 17.7 %all-to-all-start.1 = ((bf16[256,4,256]{0,2,1:T(8,128)(2,1)}), bf16[256,4,256]{0,2,1:T(8,128)(2,1)S(1)}, u32[]{:S(2)}, u32[]{:S(2)}) async-start(bf16[256,4,256]{0,2,1:T(8,128)(2,1)} %bitcast.193), calls=%async_computation.1 | async-start | bytes 1048576 | tf_op jit(solution)/shard_map/all_to_all | solution.py:60
  83.0 15.0 %collective-permute-start.6 = (bf16[1024,256]{0,1:T(8,128)(2,1)}, bf16[1024,256]{0,1:T(8,128)(2,1)}, u32[]{:S(2)}, u32[]{:S(2)}) collective-permute-start(bf16[1024,256]{0,1:T(8,128)(2,1)} %get-tuple-element.19), channel_id=1, source_target_pairs={{4,0},{8,4},{12,8},{16,12},{20,16},{24,20},{28,24},{0,28},{5,1},{9... | collective-permute-start | bytes 1572872 | tf_op jit(solution)/shard_map/ppermute | solution.py:30
  83.4 14.6 %collective-permute-start.7 = (bf16[1024,256]{0,1:T(8,128)(2,1)}, bf16[1024,256]{0,1:T(8,128)(2,1)}, u32[]{:S(2)}, u32[]{:S(2)}) collective-permute-start(bf16[1024,256]{0,1:T(8,128)(2,1)} %get-tuple-element.19), channel_id=1, source_target_pairs={{0,4},{4,8},{8,12},{12,16},{16,20},{20,24},{24,28},{28,0},{1,5},{5... | collective-permute-start | bytes 1572872 | tf_op jit(solution)/shard_map/ppermute | solution.py:29
  91.1 17.4 %all-to-all-start = ((bf16[256,4,256]{0,2,1:T(8,128)(2,1)}), bf16[256,4,256]{0,2,1:T(8,128)(2,1)S(1)}, u32[]{:S(2)}, u32[]{:S(2)}) async-start(bf16[256,4,256]{0,2,1:T(8,128)(2,1)} %bitcast.7), calls=%async_computation | async-start | bytes 1048576 | tf_op jit(solution)/shard_map/all_to_all | solution.py:60
  103.3 14.3 %collective-permute-start.8 = (bf16[1024,256]{0,1:T(8,128)(2,1)}, bf16[1024,256]{0,1:T(8,128)(2,1)}, u32[]{:S(2)}, u32[]{:S(2)}) collective-permute-start(bf16[1024,256]{0,1:T(8,128)(2,1)} %get-tuple-element.21), channel_id=1, source_target_pairs={{4,0},{8,4},{12,8},{16,12},{20,16},{24,20},{28,24},{0,28},{5,1},{9... | collective-permute-start | bytes 1572872 | tf_op jit(solution)/shard_map/ppermute | solution.py:30
  103.3 14.3 %collective-permute-start.9 = (bf16[1024,256]{0,1:T(8,128)(2,1)}, bf16[1024,256]{0,1:T(8,128)(2,1)}, u32[]{:S(2)}, u32[]{:S(2)}) collective-permute-start(bf16[1024,256]{0,1:T(8,128)(2,1)} %get-tuple-element.21), channel_id=1, source_target_pairs={{0,4},{4,8},{8,12},{12,16},{16,20},{20,24},{24,28},{28,0},{1,5},{5... | collective-permute-start | bytes 1572872 | tf_op jit(solution)/shard_map/ppermute | solution.py:29
where the time goes:
time: 145 us; the launch traced here: 144 us
  waiting for transfers between devices  40.5 us (28%)
  blocking collectives  38.4 us (26%)
  local copies, waits for them, and re-layouts  24.9 us (17%)
  starting transfers between devices  17.5 us (12%)
  matrix products  14.2 us (10%)
  other arithmetic  8.64 us (6%)
    ppermute x5, waiting for transfers between devices, shifted(): lax.ppermute(cells, axis, [((i + 1) % count, i) for i in range(count)])  32.5 us
    all_to_all x1, blocking collectives, per_device(): lax.all_to_all(current.astype(jnp.bfloat16), 'gy', split_axis=0, concat_a...  19.6 us
    all_to_all x1, blocking collectives, per_device(): lax.all_to_all(field, 'gy', split_axis=1, concat_axis=0, tiled=True)  18.7 us
    dot_general x3, matrix products, per_device(): current = jnp.dot(synthesis, scaled, preferred_element_type=jnp.float32)  14.2 us
    unnamed x16, local copies, waits for them, and re-layouts  13.8 us
    ppermute x5, starting transfers between devices, shifted(): lax.ppermute(cells, axis, [(i, (i + 1) % count) for i in range(count)])  9.53 us
    all_to_all x2, waiting for transfers between devices, per_device(): lax.all_to_all(field, 'gy', split_axis=1, concat_axis=0, tiled=True)  8.01 us
    all_to_all x2, starting transfers between devices, per_device(): lax.all_to_all(field, 'gy', split_axis=1, concat_axis=0, tiled=True)  6.94 us
  transfers between devices with their start and end apart: 12, of which 7 were waited for; matrix products, arithmetic and copies ran while one was open for 17% of the time, Pallas kernels for 0%

commit v1 on v0

--- a/solution.py
+++ b/solution.py
@@ -3,6 +3,13 @@
 import jax.numpy as jnp
 from jax import lax
 from jax.sharding import PartitionSpec as P
+
+
+def stacked_exchange(value, axis, split, join):
+    size = lax.axis_size(axis)
+    tiles = jnp.stack(jnp.split(value, size, axis=split), axis=0)
+    tiles = lax.all_to_all(tiles, axis, split_axis=0, concat_axis=0)
+    return jnp.concatenate(tiles, axis=join)
 
 
 def spectral_weights():
@@ -56,9 +63,7 @@
             local = local + prov[0]
         local = local - half_speed_part * shifted(mixed.astype(jnp.bfloat16), "gx")
         known.append(local.astype(jnp.bfloat16))
-    known = [
-        lax.all_to_all(field, "gy", split_axis=1, concat_axis=0, tiled=True) for field in known
-    ]
+    known = [stacked_exchange(field, "gy", 1, 0) for field in known]
     for m in range(3):
         rhs = known[m].astype(jnp.float32)
         if m:

time: 145 us -> 131 us (0.903)
  the two profiles are of different devices: /device:TPU:3 before, /device:TPU:0 now
where the time goes in v1:
time: 131 us
  waiting for transfers between devices  48.6 us (37%)
  starting transfers between devices  26.3 us (20%)
  blocking collectives  19.5 us (15%)
  other arithmetic  16.9 us (13%)
  matrix products  13.8 us (11%)
  local copies, waits for them, and re-layouts  5.68 us (4%)
    ppermute x5, waiting for transfers between devices, shifted(): lax.ppermute(cells, axis, [(i, (i + 1) % count) for i in range(count)])  34.1 us
    all_to_all x1, blocking collectives, per_device(): lax.all_to_all(current.astype(jnp.bfloat16), 'gy', split_axis=0, concat_a...  19.5 us
    dot_general x3, matrix products, per_device(): current = jnp.dot(synthesis, scaled, preferred_element_type=jnp.float32)  13.8 us
    all_to_all x3, waiting for transfers between devices, stacked_exchange(): tiles = lax.all_to_all(tiles, axis, split_axis=0, concat_axis=0)  12.8 us
    all_to_all x3, starting transfers between devices, stacked_exchange(): tiles = lax.all_to_all(tiles, axis, split_axis=0, concat_axis=0)  12.1 us
    ppermute x5, starting transfers between devices, shifted(): lax.ppermute(cells, axis, [((i + 1) % count, i) for i in range(count)])  10.3 us
    convert_element_type x2, other arithmetic, per_device(): local = local - half_speed_part * shifted(mixed.astype(jnp.bfloat16), 'gx')  6.69 us
    convert_element_type x2, other arithmetic, per_device(): known.append(local.astype(jnp.bfloat16))  5.29 us
  transfers between devices with their start and end apart: 13, of which 8 were waited for; matrix products, arithmetic and copies ran while one was open for 17% of the time, Pallas kernels for 0%

profile of v1, /device:TPU:0, one launch (start us, length us, event | category | flops | bytes accessed | tf_op | source)
XLA Modules:
  0.0 130.9 jit_solution(2550933628894934486)
XLA Ops:
  0.0 0.0 copy-start
  0.0 2.9 %fusion.82 = bf16[256,1024]{1,0:T(8,128)(2,1)} fusion(bf16[4,1,256,1024]{3,2,1,0:T(8,128)(2,1)} %param.8), kind=kLoop, calls=%fused_computation.127 | loop fusion | flops 3145728 | bytes 2621440 | tf_op jit(solution)/shard_map/convert_element_type | solution.py:64
  2.9 0.5 collective-permute-start.5
  3.4 2.9 %collective-permute-start.4 = (bf16[256,1024]{1,0:T(8,128)(2,1)}, bf16[256,1024]{1,0:T(8,128)(2,1)S(1)}, u32[]{:S(2)}, u32[]{:S(2)}) collective-permute-start(bf16[256,1024]{1,0:T(8,128)(2,1)} %fusion.82), channel_id=1, source_target_pairs={{4,0},{8,4},{12,8},{16,12},{20,16},{24,20},{28,24},{0,28},{5,1},{9... | collective-permute-start | bytes 1572872 | tf_op jit(solution)/shard_map/ppermute | solution.py:37
  6.3 10.0 %collective-permute-done.5 = bf16[256,1024]{1,0:T(8,128)(2,1)S(1)} collective-permute-done((bf16[256,1024]{1,0:T(8,128)(2,1)}, bf16[256,1024]{1,0:T(8,128)(2,1)S(1)}, u32[]{:S(2)}, u32[]{:S(2)}) %collective-permute-start.5) | collective-permute-done | bytes 524320 | tf_op jit(solution)/shard_map/ppermute | solution.py:36
  16.3 1.6 %collective-permute-done.4 = bf16[256,1024]{1,0:T(8,128)(2,1)S(1)} collective-permute-done((bf16[256,1024]{1,0:T(8,128)(2,1)}, bf16[256,1024]{1,0:T(8,128)(2,1)S(1)}, u32[]{:S(2)}, u32[]{:S(2)}) %collective-permute-start.4) | collective-permute-done | bytes 524320 | tf_op jit(solution)/shard_map/ppermute | solution.py:37
  17.9 3.8 %fusion.84 = (bf16[256,1024]{1,0:T(8,128)(2,1)S(1)}, bf16[256,1024]{1,0:T(8,128)(2,1)S(1)}) fusion(bf16[4,1,256,1024]{3,2,1,0:T(8,128)(2,1)} %param.8, bf16[256,1024]{1,0:T(8,128)(2,1)S(1)} %collective-permute-done.5, bf16[256,1024]{1,0:T(8,128)(2,1)S(1)} %collective-permute-done.4, f32[256]{0:T(256)S(1)} %bitcast.213, f32[256]{0:T(256)S(1)} %bitcast.216, ...), kind=kLoop, calls=%fused_computation.129 | loop fusion | flops 10223616 | bytes 6293504 | tf_op jit(solution)/shard_map/convert_element_type | solution.py:64
  21.7 1.7 %collective-permute-start.1 = (bf16[256,1024]{1,0:T(8,128)(2,1)S(1)}, bf16[256,1024]{1,0:T(8,128)(2,1)S(1)}, u32[]{:S(2)}, u32[]{:S(2)}) collective-permute-start(bf16[256,1024]{1,0:T(8,128)(2,1)S(1)} %get-tuple-element.7), channel_id=1, source_target_pairs={{0,4},{4,8},{8,12},{12,16},{16,20},{20,24},{24,28},{28,0},{1,5},{5... | collective-permute-start | bytes 1572872 | tf_op jit(solution)/shard_map/ppermute | solution.py:36
  23.4 1.1 collective-permute-start
  24.5 11.6 %collective-permute-done.1 = bf16[256,1024]{1,0:T(8,128)(2,1)S(1)} collective-permute-done((bf16[256,1024]{1,0:T(8,128)(2,1)S(1)}, bf16[256,1024]{1,0:T(8,128)(2,1)S(1)}, u32[]{:S(2)}, u32[]{:S(2)}) %collective-permute-start.1) | collective-permute-done | bytes 524320 | tf_op jit(solution)/shard_map/ppermute | solution.py:36
  36.1 0.0 collective-permute-done
  36.1 0.0 copy-done.1
  36.1 1.5 %fusion.17 = (bf16[256,1024]{1,0:T(8,128)(2,1)S(1)}, bf16[256,1024]{1,0:T(8,128)(2,1)S(1)}) fusion(bf16[256,1024]{1,0:T(8,128)(2,1)S(1)} %collective-permute-done.1, bf16[256,1024]{1,0:T(8,128)(2,1)S(1)} %collective-permute-done, f32[256]{0:T(256)S(1)} %bitcast.214, f32[256]{0:T(256)S(1)} %bitcast.217, bf16[4,1,256,1024]{3,2,1,0:T(8,128)(2,1)S(1)} %copy-done.2, ...), kind=kLoop, calls=%fused_computation.49 | loop fusion | flops 9961472 | bytes 6293504 | tf_op jit(solution)/shard_map/convert_element_type | solution.py:65
  37.6 1.6 %collective-permute-start.3 = (bf16[256,1024]{1,0:T(8,128)(2,1)S(1)}, bf16[256,1024]{1,0:T(8,128)(2,1)}, u32[]{:S(2)}, u32[]{:S(2)}) collective-permute-start(bf16[256,1024]{1,0:T(8,128)(2,1)S(1)} %get-tuple-element.6), channel_id=1, source_target_pairs={{0,4},{4,8},{8,12},{12,16},{16,20},{20,24},{24,28},{28,0},{1,5},{5... | collective-permute-start | bytes 1572872 | tf_op jit(solution)/shard_map/ppermute | solution.py:36
  39.3 1.1 collective-permute-start.2
  40.4 0.9 pad_maximum_fusion.2
  41.2 4.5 %all-to-all-start.2 = ((bf16[4,256,256]{2,1,0:T(8,128)(2,1)}), bf16[4,256,256]{2,1,0:T(8,128)(2,1)}, u32[]{:S(2)}, u32[]{:S(2)}) async-start(bf16[4,256,256]{2,1,0:T(8,128)(2,1)} %pad_maximum_fusion.2), calls=%async_computation.2 | async-start | bytes 1048576 | tf_op jit(solution)/shard_map/all_to_all | solution.py:11
  45.7 0.8 dynamic_slice.11
  46.5 6.1 %collective-permute-done.3 = bf16[256,1024]{1,0:T(8,128)(2,1)} collective-permute-done((bf16[256,1024]{1,0:T(8,128)(2,1)S(1)}, bf16[256,1024]{1,0:T(8,128)(2,1)}, u32[]{:S(2)}, u32[]{:S(2)}) %collective-permute-start.3) | collective-permute-done | bytes 524320 | tf_op jit(solution)/shard_map/ppermute | solution.py:36
  52.6 0.0 collective-permute-done.2
  52.6 3.8 %fusion.24 = bf16[256,1024]{1,0:T(8,128)(2,1)S(1)} fusion(bf16[256,1024]{1,0:T(8,128)(2,1)} %collective-permute-done.3, bf16[256,1024]{1,0:T(8,128)(2,1)} %collective-permute-done.2, f32[256]{0:T(256)S(1)} %bitcast.215, f32[256]{0:T(256)S(1)} %bitcast.218, bf16[4,1,256,1024]{3,2,1,0:T(8,128)(2,1)} %param.9, bf16[4,1,256,1024]{3,2,1,0:T(8,128)(2,1)} %param.8), kind=kLoop, calls=%fused_computation.56 | loop fusion | flops 7864320 | bytes 5769216 | tf_op jit(solution)/shard_map/convert_element_type | solution.py:65
  56.4 0.0 copy-start.6
  56.4 0.9 pad_maximum_fusion.1
  57.3 3.0 %all-to-all-done.2 = bf16[4,256,256]{2,1,0:T(8,128)(2,1)} async-done(((bf16[4,256,256]{2,1,0:T(8,128)(2,1)}), bf16[4,256,256]{2,1,0:T(8,128)(2,1)}, u32[]{:S(2)}, u32[]{:S(2)}) %all-to-all-start.2) | async-done | bytes 524320 | tf_op jit(solution)/shard_map/all_to_all | solution.py:11
  60.3 3.5 %all-to-all-start.1 = ((bf16[4,256,256]{2,1,0:T(8,128)(2,1)}), bf16[4,256,256]{2,1,0:T(8,128)(2,1)S(1)}, u32[]{:S(2)}, u32[]{:S(2)}) async-start(bf16[4,256,256]{2,1,0:T(8,128)(2,1)} %pad_maximum_fusion.1), calls=%async_computation.1 | async-start | bytes 1048576 | tf_op jit(solution)/shard_map/all_to_all | solution.py:11
  63.8 4.4 %fusion.85 = (bf16[1024,256]{0,1:T(8,128)(2,1)}, f32[1024,256]{0,1:T(8,128)}) fusion(bf16[1024,1024]{1,0:T(8,128)(2,1)S(1)} %copy-done, bf16[1024,256]{1,0:T(8,128)(2,1)} %bitcast.30, bf16[1024,1024]{1,0:T(8,128)(2,1)} %param.14, f32[256]{0:T(256)S(1)} %dynamic_slice.11, f32[1024]{0:T(1024)S(1)} %copy-done.6), kind=kOutput, calls=%fused_computation.130 | convolution fusion | flops 1075576832 | bytes 6296576 | tf_op jit(solution)/shard_map/dot_general | solution.py:81
  68.2 0.0 collective-permute-start.7
  68.2 2.6 %collective-permute-start.6 = (bf16[1024,256]{0,1:T(8,128)(2,1)}, bf16[1024,256]{0,1:T(8,128)(2,1)}, u32[]{:S(2)}, u32[]{:S(2)}) collective-permute-start(bf16[1024,256]{0,1:T(8,128)(2,1)} %get-tuple-element.21), channel_id=1, source_target_pairs={{4,0},{8,4},{12,8},{16,12},{20,16},{24,20},{28,24},{0,28},{5,1},{9... | collective-permute-start | bytes 1572872 | tf_op jit(solution)/shard_map/ppermute | solution.py:37
  70.8 0.9 pad_maximum_fusion
  71.7 6.0 %all-to-all-done.1 = bf16[4,256,256]{2,1,0:T(8,128)(2,1)S(1)} async-done(((bf16[4,256,256]{2,1,0:T(8,128)(2,1)}), bf16[4,256,256]{2,1,0:T(8,128)(2,1)S(1)}, u32[]{:S(2)}, u32[]{:S(2)}) %all-to-all-start.1) | async-done | bytes 524320 | tf_op jit(solution)/shard_map/all_to_all | solution.py:11
  77.7 0.8 copy-done.3
  78.6 4.1 %all-to-all-start = ((bf16[4,256,256]{2,1,0:T(8,128)(2,1)}), bf16[4,256,256]{2,1,0:T(8,128)(2,1)}, u32[]{:S(2)}, u32[]{:S(2)}) async-start(bf16[4,256,256]{2,1,0:T(8,128)(2,1)} %pad_maximum_fusion), calls=%async_computation | async-start | bytes 1048576 | tf_op jit(solution)/shard_map/all_to_all | solution.py:11
  82.7 1.1 bitcast_convert_fusion
  83.8 1.3 copy.17
  85.1 0.0 collective-permute-done.7
  85.1 0.0 collective-permute-done.6
  85.2 5.3 %fusion.86 = (bf16[1024,256]{0,1:T(8,128)(2,1)}, f32[1024,256]{0,1:T(8,128)}) fusion(bf16[1024,1024]{1,0:T(8,128)(2,1)S(1)} %copy-done, bf16[1024,1024]{1,0:T(8,128)(2,1)} %param.14, bf16[1024,256]{0,1:T(8,128)(2,1)} %collective-permute-done.7, bf16[1024,256]{0,1:T(8,128)(2,1)} %collective-permute-done.6, bf16[1024,256]{0,1:T(8,128)(2,1)} %get-tuple-element.21, ...), kind=kOutput, calls=%fused_computation.131 | convolution fusion | flops 1078460416 | bytes 9450496 | tf_op jit(solution)/shard_map/dot_general | solution.py:81
  90.4 0.0 collective-permute-start.9
  90.4 2.6 %collective-permute-start.8 = (bf16[1024,256]{0,1:T(8,128)(2,1)}, bf16[1024,256]{0,1:T(8,128)(2,1)}, u32[]{:S(2)}, u32[]{:S(2)}) collective-permute-start(bf16[1024,256]{0,1:T(8,128)(2,1)} %get-tuple-element.23), channel_id=1, source_target_pairs={{4,0},{8,4},{12,8},{16,12},{20,16},{24,20},{28,24},{0,28},{5,1},{9... | collective-permute-start | bytes 1572872 | tf_op jit(solution)/shard_map/ppermute | solution.py:37
  93.1 3.8 %all-to-all-done = bf16[4,256,256]{2,1,0:T(8,128)(2,1)} async-done(((bf16[4,256,256]{2,1,0:T(8,128)(2,1)}), bf16[4,256,256]{2,1,0:T(8,128)(2,1)}, u32[]{:S(2)}, u32[]{:S(2)}) %all-to-all-start) | async-done | bytes 524320 | tf_op jit(solution)/shard_map/all_to_all | solution.py:11
  96.9 1.1 bitcast_convert_fusion.1
  98.0 1.3 copy.16
  99.3 6.5 %collective-permute-done.9 = bf16[1024,256]{0,1:T(8,128)(2,1)} collective-permute-done((bf16[1024,256]{0,1:T(8,128)(2,1)}, bf16[1024,256]{0,1:T(8,128)(2,1)}, u32[]{:S(2)}, u32[]{:S(2)}) %collective-permute-start.9) | collective-permute-done | bytes 524320 | tf_op jit(solution)/shard_map/ppermute | solution.py:36
  105.8 0.0 collective-permute-done.8
  105.8 4.1 %convolution_convert_fusion = bf16[256,1024]{1,0:T(8,128)(2,1)S(1)} fusion(bf16[1024,1024]{1,0:T(8,128)(2,1)S(1)} %copy-done, bf16[1024,1024]{1,0:T(8,128)(2,1)} %param.14, bf16[1024,256]{0,1:T(8,128)(2,1)} %collective-permute-done.9, bf16[1024,256]{0,1:T(8,128)(2,1)} %collective-permute-done.8, bf16[1024,256]{0,1:T(8,128)(2,1)} %get-tuple-element.23, ...), kind=kOutput, calls=%fused_computation.35 | convolution fusion | flops 1078460416 | bytes 8401920 | tf_op jit(solution)/shard_map/dot_general | solution.py:81
  110.0 19.5 %all_to_all.28 = bf16[4,256,256]{1,2,0:T(8,128)(2,1)S(1)} all-to-all(bf16[4,256,256]{1,2,0:T(8,128)(2,1)S(1)} %bitcast.211), channel_id=1, replica_groups=mesh['gx'=8,'gy'=4] {'gy'}, dimensions={0} | all-to-all | bytes 1048576 | tf_op jit(solution)/shard_map/all_to_all | solution.py:82
  129.5 0.1 convert_element_type.192
  129.6 1.3 copy.15
  (16 shorter events, 0.2 us)
Async XLA Ops:
  0.0 63.8 %copy-start = (bf16[1024,1024]{1,0:T(8,128)(2,1)S(1)}, bf16[1024,1024]{1,0:T(8,128)(2,1)}, u32[]{:S(2)}) copy-start(bf16[1024,1024]{1,0:T(8,128)(2,1)} %param.15) | copy-start | bytes 6291460
  0.0 6.2 %copy-start.4 = (f32[1,1024]{1,0:T(1,128)S(1)}, f32[1,1024]{1,0:T(1,128)}, u32[]{:S(2)}) copy-start(f32[1,1024]{1,0:T(1,128)} %param.10) | copy-start | bytes 12292
  0.0 6.2 %copy-start.5 = (f32[1,1024]{1,0:T(1,128)S(1)}, f32[1,1024]{1,0:T(1,128)}, u32[]{:S(2)}) copy-start(f32[1,1024]{1,0:T(1,128)} %param.11) | copy-start | bytes 12292
  2.9 13.4 %collective-permute-start.5 = (bf16[256,1024]{1,0:T(8,128)(2,1)}, bf16[256,1024]{1,0:T(8,128)(2,1)S(1)}, u32[]{:S(2)}, u32[]{:S(2)}) collective-permute-start(bf16[256,1024]{1,0:T(8,128)(2,1)} %fusion.82), channel_id=1, source_target_pairs={{0,4},{4,8},{8,12},{12,16},{16,20},{20,24},{24,28},{28,0},{1,5},{5... | collective-permute-start | bytes 1572872 | tf_op jit(solution)/shard_map/ppermute | solution.py:36
  3.4 14.5 %collective-permute-start.4 = (bf16[256,1024]{1,0:T(8,128)(2,1)}, bf16[256,1024]{1,0:T(8,128)(2,1)S(1)}, u32[]{:S(2)}, u32[]{:S(2)}) collective-permute-start(bf16[256,1024]{1,0:T(8,128)(2,1)} %fusion.82), channel_id=1, source_target_pairs={{4,0},{8,4},{12,8},{16,12},{20,16},{24,20},{28,24},{0,28},{5,1},{9... | collective-permute-start | bytes 1572872 | tf_op jit(solution)/shard_map/ppermute | solution.py:37
  17.9 18.2 %copy-start.1 = (bf16[4,1,256,1024]{3,2,1,0:T(8,128)(2,1)S(1)}, bf16[4,1,256,1024]{3,2,1,0:T(8,128)(2,1)}, u32[]{:S(2)}) copy-start(bf16[4,1,256,1024]{3,2,1,0:T(8,128)(2,1)} %param.8) | copy-start | bytes 6291460
  17.9 18.2 %copy-start.2 = (bf16[4,1,256,1024]{3,2,1,0:T(8,128)(2,1)S(1)}, bf16[4,1,256,1024]{3,2,1,0:T(8,128)(2,1)}, u32[]{:S(2)}) copy-start(bf16[4,1,256,1024]{3,2,1,0:T(8,128)(2,1)} %param.9) | copy-start | bytes 6291460
  21.7 14.4 %collective-permute-start.1 = (bf16[256,1024]{1,0:T(8,128)(2,1)S(1)}, bf16[256,1024]{1,0:T(8,128)(2,1)S(1)}, u32[]{:S(2)}, u32[]{:S(2)}) collective-permute-start(bf16[256,1024]{1,0:T(8,128)(2,1)S(1)} %get-tuple-element.7), channel_id=1, source_target_pairs={{0,4},{4,8},{8,12},{12,16},{16,20},{20,24},{24,28},{28,0},{1,5},{5... | collective-permute-start | bytes 1572872 | tf_op jit(solution)/shard_map/ppermute | solution.py:36
  23.4 12.7 %collective-permute-start = (bf16[256,1024]{1,0:T(8,128)(2,1)S(1)}, bf16[256,1024]{1,0:T(8,128)(2,1)S(1)}, u32[]{:S(2)}, u32[]{:S(2)}) collective-permute-start(bf16[256,1024]{1,0:T(8,128)(2,1)S(1)} %get-tuple-element.7), channel_id=1, source_target_pairs={{4,0},{8,4},{12,8},{16,12},{20,16},{24,20},{28,24},{0,28},{5,1},{9... | collective-permute-start | bytes 1572872 | tf_op jit(solution)/shard_map/ppermute | solution.py:37
  37.6 15.0 %collective-permute-start.3 = (bf16[256,1024]{1,0:T(8,128)(2,1)S(1)}, bf16[256,1024]{1,0:T(8,128)(2,1)}, u32[]{:S(2)}, u32[]{:S(2)}) collective-permute-start(bf16[256,1024]{1,0:T(8,128)(2,1)S(1)} %get-tuple-element.6), channel_id=1, source_target_pairs={{0,4},{4,8},{8,12},{12,16},{16,20},{20,24},{24,28},{28,0},{1,5},{5... | collective-permute-start | bytes 1572872 | tf_op jit(solution)/shard_map/ppermute | solution.py:36
  39.3 13.3 %collective-permute-start.2 = (bf16[256,1024]{1,0:T(8,128)(2,1)S(1)}, bf16[256,1024]{1,0:T(8,128)(2,1)}, u32[]{:S(2)}, u32[]{:S(2)}) collective-permute-start(bf16[256,1024]{1,0:T(8,128)(2,1)S(1)} %get-tuple-element.6), channel_id=1, source_target_pairs={{4,0},{8,4},{12,8},{16,12},{20,16},{24,20},{28,24},{0,28},{5,1},{9... | collective-permute-start | bytes 1572872 | tf_op jit(solution)/shard_map/ppermute | solution.py:37
  41.2 19.1 %all-to-all-start.2 = ((bf16[4,256,256]{2,1,0:T(8,128)(2,1)}), bf16[4,256,256]{2,1,0:T(8,128)(2,1)}, u32[]{:S(2)}, u32[]{:S(2)}) async-start(bf16[4,256,256]{2,1,0:T(8,128)(2,1)} %pad_maximum_fusion.2), calls=%async_computation.2 | async-start | bytes 1048576 | tf_op jit(solution)/shard_map/all_to_all | solution.py:11
  56.4 7.4 %copy-start.6 = (f32[1024]{0:T(1024)S(1)}, f32[1024]{0:T(1024)}, u32[]{:S(2)}) copy-start(f32[1024]{0:T(1024)} %param.12) | copy-start | bytes 12292
  60.3 17.4 %all-to-all-start.1 = ((bf16[4,256,256]{2,1,0:T(8,128)(2,1)}), bf16[4,256,256]{2,1,0:T(8,128)(2,1)S(1)}, u32[]{:S(2)}, u32[]{:S(2)}) async-start(bf16[4,256,256]{2,1,0:T(8,128)(2,1)} %pad_maximum_fusion.1), calls=%async_computation.1 | async-start | bytes 1048576 | tf_op jit(solution)/shard_map/all_to_all | solution.py:11
  68.2 17.0 %collective-permute-start.7 = (bf16[1024,256]{0,1:T(8,128)(2,1)}, bf16[1024,256]{0,1:T(8,128)(2,1)}, u32[]{:S(2)}, u32[]{:S(2)}) collective-permute-start(bf16[1024,256]{0,1:T(8,128)(2,1)} %get-tuple-element.21), channel_id=1, source_target_pairs={{0,4},{4,8},{8,12},{12,16},{16,20},{20,24},{24,28},{28,0},{1,5},{5... | collective-permute-start | bytes 1572872 | tf_op jit(solution)/shard_map/ppermute | solution.py:36
  68.2 17.0 %collective-permute-start.6 = (bf16[1024,256]{0,1:T(8,128)(2,1)}, bf16[1024,256]{0,1:T(8,128)(2,1)}, u32[]{:S(2)}, u32[]{:S(2)}) collective-permute-start(bf16[1024,256]{0,1:T(8,128)(2,1)} %get-tuple-element.21), channel_id=1, source_target_pairs={{4,0},{8,4},{12,8},{16,12},{20,16},{24,20},{28,24},{0,28},{5,1},{9... | collective-permute-start | bytes 1572872 | tf_op jit(solution)/shard_map/ppermute | solution.py:37
  77.7 0.8 copy-start.3
  78.6 18.3 %all-to-all-start = ((bf16[4,256,256]{2,1,0:T(8,128)(2,1)}), bf16[4,256,256]{2,1,0:T(8,128)(2,1)}, u32[]{:S(2)}, u32[]{:S(2)}) async-start(bf16[4,256,256]{2,1,0:T(8,128)(2,1)} %pad_maximum_fusion), calls=%async_computation | async-start | bytes 1048576 | tf_op jit(solution)/shard_map/all_to_all | solution.py:11
  90.4 15.3 %collective-permute-start.9 = (bf16[1024,256]{0,1:T(8,128)(2,1)}, bf16[1024,256]{0,1:T(8,128)(2,1)}, u32[]{:S(2)}, u32[]{:S(2)}) collective-permute-start(bf16[1024,256]{0,1:T(8,128)(2,1)} %get-tuple-element.23), channel_id=1, source_target_pairs={{0,4},{4,8},{8,12},{12,16},{16,20},{20,24},{24,28},{28,0},{1,5},{5... | collective-permute-start | bytes 1572872 | tf_op jit(solution)/shard_map/ppermute | solution.py:36
  90.4 15.3 %collective-permute-start.8 = (bf16[1024,256]{0,1:T(8,128)(2,1)}, bf16[1024,256]{0,1:T(8,128)(2,1)}, u32[]{:S(2)}, u32[]{:S(2)}) collective-permute-start(bf16[1024,256]{0,1:T(8,128)(2,1)} %get-tuple-element.23), channel_id=1, source_target_pairs={{4,0},{8,4},{12,8},{16,12},{20,16},{24,20},{28,24},{0,28},{5,1},{9... | collective-permute-start | bytes 1572872 | tf_op jit(solution)/shard_map/ppermute | solution.py:37
